TPU v7x, 256 devices: a whole 4x4x8 slice. The times are simulated.
256 devices in a mesh: gx: 32 (over x, y, core), gy: 8 (over z).
Axes of the slice: x: 4, y: 4, z: 8, core: 2. Of those that a mesh axis runs over, the one named last changes fastest.
Arguments:
- eastward: float32 [256, 1024, 128], P('gx', 'gy'), may hold values from -6 to 6
- northward: float32 [256, 1024, 128], P('gx', 'gy'), may hold values from -6 to 6
- vertical: float32 [256, 1024, 128], P('gx', 'gy'), may hold values from -6 to 6
- pressure: float32 [256, 1024, 128], P('gx', 'gy'), may hold values from -6 to 6
- theta: float32 [256, 1024, 128], P('gx', 'gy'), may hold values from -6 to 6
- humidity: float32 [256, 1024, 128], P('gx', 'gy'), may hold values from 0.95 to 1.07
- sound_speed: float32 [128], replicated, may hold values from 0.25 to 1
- radius_sq: float32 [64, 8, 256, 1024], P(None, None, 'gx', 'gy'), may hold values from 0.25 to 4
- multiplicity: bfloat16 [64, 8, 256, 1024], P(None, None, 'gx', 'gy'), may hold values from 0.5 to 2
- droplet_count: int32 [8, 256, 1024], P(None, 'gx', 'gy'), may hold values from 0 to 64
Outputs:
- eastward_out: float32 [256, 1024, 128], P('gx', 'gy')
- northward_out: float32 [256, 1024, 128], P('gx', 'gy')
- vertical_out: float32 [256, 1024, 128], P('gx', 'gy')
- pressure_out: float32 [256, 1024, 128], P('gx', 'gy')
- theta_out: float32 [256, 1024, 128], P('gx', 'gy')
- humidity_out: float32 [256, 1024, 128], P('gx', 'gy')
- radius_out: float32 [64, 8, 256, 1024], P(None, None, 'gx', 'gy')
- saturation_profile: float32 [128], replicated
All inputs are finite; a program needn't handle non-finite values.
Results may differ from a plain program's by a relative error of at most 0.0003.
Values sent between devices are 32-bit elements; how exact they have to be, the bound alone decides.
A program may use at most 64 MiB of HBM per device.

v0:
```python
import functools

import jax
import jax.numpy as jnp
from jax import lax
from jax.experimental import pallas as pl
from jax.experimental.pallas import tpu as pltpu
from jax.sharding import PartitionSpec as P

F32 = jnp.float32
BF16 = jnp.bfloat16
MESH = pl.DeviceIdType.MESH
X, Y, Z = 8, 128, 128
SLOTS, CLOUD, BASE = 64, 8, 32
ROWS = CLOUD * X
CHUNKS = 8
PER = SLOTS // CHUNKS
TOP = 8
SLOPE, GROWTH, FLOOR, MASS, LATENT, BUOYANCY = 0.01, 25.0, 0.0625, 0.0004, 200.0, 0.5


def split(x):
    high = x.astype(BF16)
    return high, (x - high.astype(F32)).astype(BF16)


def mm(a, b):
    return jnp.dot(a, b, preferred_element_type=F32)


def times(x, high, low):
    xh, xl = split(x)
    return mm(xh, high) + (mm(xl, high) + mm(xh, low))


def solve(forcing, explicit, high, low):
    both = times(jnp.concatenate([forcing, explicit], axis=1), high, low)
    return both[:, :Z], explicit + both[:, Z:]


def move_east(p, e_in, e_out, first, last):
    own = slice(TOP, TOP + Y)
    for a in range(first, last):
        e_out[a] = e_in[a] - 0.5 * (p[a + 2, own, :] - p[a, own, :])


def move_north(p, n_in, n_out, first, last):
    for i in range(X):
        n_out[i, first:last, :] = n_in[i, first:last, :] - 0.5 * (
            p[i + 2, first + 1 : last + 1, :] - p[i + 2, first - 1 : last - 1, :]
        )


def explicit_pressure(p, e, n, c, i):
    spread = 0.5 * (
        (e[i + 2] - e[i]) + (n[i, TOP + 1 : TOP + Y + 1, :] - n[i, TOP - 1 : TOP + Y - 1, :])
    )
    return p[i + 2, TOP : TOP + Y, :] - c * spread


def edges_north(p, n_in, n_out):
    move_north(p, n_in, n_out, TOP - 1, TOP)
    move_north(p, n_in, n_out, TOP, TOP + 8)
    move_north(p, n_in, n_out, TOP + Y - 8, TOP + Y)
    move_north(p, n_in, n_out, TOP + Y, TOP + Y + 1)


def column_matrix(c):
    k = lax.broadcasted_iota(jnp.int32, (Z, Z), 0)
    j = lax.broadcasted_iota(jnp.int32, (Z, Z), 1)
    here = jnp.broadcast_to(c, (Z, Z))
    above = pltpu.roll(here, Z - 1, 1)
    m = jnp.where(k == j, 1.0 + jnp.where(k < Z - 1, here + above, 0.0), 0.0)
    m = m - jnp.where((j == k + 1) & (j < Z - 1), here, 0.0)
    m = m - jnp.where((j == k - 1) & (k < Z - 1), above, 0.0)
    eye = jnp.where(k == j, 1.0, 0.0)
    return eye, eye - m * (1.0 / 3.0)


def column_tables(inverse, c):
    k = lax.broadcasted_iota(jnp.int32, (Z, Z), 0)
    a = jnp.where(k < Z - 1, inverse, 0.0)
    b = a - pltpu.roll(a, 1, 0)
    left = jnp.concatenate([a, b], axis=0)
    j = lax.broadcasted_iota(jnp.int32, (2 * Z, Z), 1)
    m = jnp.where(j < Z - 1, left, 0.0)
    right = (pltpu.roll(m, 1, 1) - m) * c
    return split(jnp.concatenate([left, right], axis=1))


def kernel_main(
    lo_size,
    e_hbm, n_hbm, v_hbm, p_hbm, th_hbm, hu_hbm, c_hbm, r_hbm, m_hbm, k_hbm,
    p2, e, n, f, th, hu, r, wh, wl, total,
    p0, p1, v, c_ref, m_ref, k_ref, cl, xr, r1, r2, r3,
    load_sem, r_sem, m_sem, hs, hr, as_, ar,
):
    gx, gy = lax.axis_index("gx"), lax.axis_index("gy")
    nx, ny = lax.axis_size("gx"), lax.axis_size("gy")
    hi_size = nx // lo_size
    lo, hi = lax.rem(gx, lo_size), gx // lo_size
    right, left = lax.rem(gx + 1, nx), lax.rem(gx + nx - 1, nx)
    up, down = lax.rem(gy + 1, ny), lax.rem(gy + ny - 1, ny)
    own = slice(TOP, TOP + Y)

    loads = []
    for at, (src, dst) in enumerate(
        (
            (th_hbm, th),
            (hu_hbm, hu),
            (k_hbm, k_ref),
            (c_hbm, c_ref),
            (p_hbm, p0.at[2:10, own, :]),
            (e_hbm, e.at[1:9]),
            (n_hbm, n.at[:, own, :]),
            (v_hbm, v),
        )
    ):
        loads.append(pltpu.make_async_copy(src, dst, load_sem.at[at]))

    def droplets(q):
        part = pl.ds(q * PER, PER)
        return (
            pltpu.make_async_copy(r_hbm.at[part], r.at[part], r_sem.at[q]),
            pltpu.make_async_copy(m_hbm.at[part], m_ref.at[part], m_sem.at[q]),
        )

    for copy in loads[:4]:
        copy.start()
    for q in range(CHUNKS):
        for copy in droplets(q):
            copy.start()
    for copy in loads[4:]:
        copy.start()

    barrier = pltpu.get_barrier_semaphore()
    peers = [(hi * lo_size + lax.rem(lo + d, lo_size), gy) for d in range(1, lo_size)]
    lo_peers = list(peers)
    hi_peers = [(lax.rem(hi + d, hi_size) * lo_size + lo, gy) for d in range(1, hi_size)]
    gy_peers = [(gx, lax.rem(gy + d, ny)) for d in range(1, ny)]
    everyone = [(left, gy), (right, gy)] + lo_peers + hi_peers + gy_peers
    for who in everyone:
        pl.semaphore_signal(barrier, inc=1, device_id=who, device_id_type=MESH)
    pl.semaphore_wait(barrier, len(everyone))

    def send(src, dst, at, who):
        return pltpu.make_async_remote_copy(
            src_ref=src,
            dst_ref=dst,
            send_sem=hs.at[at],
            recv_sem=hr.at[at],
            device_id=who,
            device_id_type=MESH,
        )

    def to_left(p, at):
        return send(p.at[2:4, own, :], p.at[10:12, own, :], at, (left, gy))

    def to_right(p, at):
        return send(p.at[8:10, own, :], p.at[0:2, own, :], at, (right, gy))

    def to_down(p, at):
        return send(p.at[2:10, TOP : TOP + 8, :], p.at[2:10, TOP + Y :, :], at, (gx, down))

    def to_up(p, at):
        return send(p.at[2:10, TOP + Y - 8 : TOP + Y, :], p.at[2:10, 0:TOP, :], at, (gx, up))

    halo0 = [
        send(p_hbm.at[0:2], p0.at[10:12, own, :], 0, (left, gy)),
        send(p_hbm.at[6:8], p0.at[0:2, own, :], 1, (right, gy)),
        send(e_hbm.at[0:1], e.at[9:10], 2, (left, gy)),
        send(e_hbm.at[7:8], e.at[0:1], 3, (right, gy)),
        send(p_hbm.at[:, 0:8, :], p0.at[2:10, TOP + Y :, :], 4, (gx, down)),
        send(p_hbm.at[:, Y - 8 :, :], p0.at[2:10, 0:TOP, :], 5, (gx, up)),
        send(n_hbm.at[:, 0:8, :], n.at[:, TOP + Y :, :], 6, (gx, down)),
        send(n_hbm.at[:, Y - 8 :, :], n.at[:, 0:TOP, :], 7, (gx, up)),
    ]
    for copy in halo0:
        copy.start()

    for copy in loads[:4]:
        copy.wait()
    c = c_ref[...]

    def saturation(i, _):
        sat = hu[i] * jnp.exp(-SLOPE * th[i]) - 1.0
        cl[:, pl.ds(i, 1), :] = GROWTH * jnp.transpose(sat)[BASE : BASE + CLOUD].reshape(CLOUD, 1, Y)
        return 0

    lax.fori_loop(0, X, saturation, 0)

    eye, r0 = column_matrix(c)
    xr[0:Z, :] = eye
    xr[Z:, :] = r0

    def condense(q, acc):
        for copy in droplets(q):
            copy.wait()
        growth = cl[...].reshape(ROWS, Y)
        count = k_ref[...].reshape(ROWS, Y)
        for s in range(PER):
            slot = q * PER + s
            old = r[slot]
            grown = jnp.maximum(old + growth, FLOOR)
            live = count > slot
            mass = m_ref[slot].astype(F32) * (
                grown * grown * lax.rsqrt(grown) - old * old * lax.rsqrt(old)
            )
            r[slot] = jnp.where(live, grown, 0.0)
            acc = acc + jnp.where(live, mass, 0.0)
        x = xr[...]
        high, low = split(x[Z:])
        product = times(x, high, low)
        xr[0:Z, :] = x[:Z] + product[:Z]
        xr[Z:, :] = product[Z:]
        return acc

    acc = lax.fori_loop(0, CHUNKS, condense, jnp.zeros((ROWS, Y), F32))
    cl[...] = (MASS * acc).reshape(CLOUD, X, Y)
    high, low = column_tables(xr[0:Z, :] * (1.0 / 3.0), c)
    wh[...] = high
    wl[...] = low

    def heating(i, sums):
        change = cl[:, pl.ds(i, 1), :].reshape(CLOUD, Y)
        added = jnp.transpose(
            jnp.concatenate(
                [jnp.zeros((BASE, Y), F32), change, jnp.zeros((Z - BASE - CLOUD, Y), F32)], axis=0
            )
        )
        wet = hu[i] - added
        warm = th[i] + LATENT * added
        hu[i] = wet
        th[i] = warm
        percent = 100.0 * (wet * jnp.exp(-SLOPE * warm) - 1.0)
        return (
            sums[0] + jnp.sum(percent.reshape(Y // 8, 8, Z), axis=0),
            sums[1] + jnp.sum(warm.reshape(Y // 8, 8, Z), axis=0),
        )

    zero = jnp.zeros((8, Z), F32)
    sums = lax.fori_loop(0, X, heating, (zero, zero))
    row = lax.broadcasted_iota(jnp.int32, (8, Z), 0)

    def gather(buffer, me, who, at):
        return [
            pltpu.make_async_remote_copy(
                src_ref=buffer.at[me],
                dst_ref=buffer.at[me],
                send_sem=as_.at[at + d],
                recv_sem=ar.at[at + d],
                device_id=peer,
                device_id_type=MESH,
            )
            for d, peer in enumerate(who)
        ]

    def add(buffer, count):
        value = buffer[0]
        for d in range(1, count):
            value = value + buffer[d]
        return value

    stage1 = gather(r1, lo, lo_peers, 0)
    stage2 = gather(r2, hi, hi_peers, len(lo_peers))
    stage3 = gather(r3, gy, gy_peers, len(lo_peers) + len(hi_peers))
    r1[lo] = jnp.where(
        row == 0,
        jnp.sum(sums[0], axis=0, keepdims=True),
        jnp.where(row == 1, jnp.sum(sums[1], axis=0, keepdims=True), 0.0),
    )
    for copy in stage1:
        copy.start()

    for copy in loads[4:]:
        copy.wait()

    def columns(p, i, count):
        forcing = jnp.concatenate([v[a] + BUOYANCY * th[a] for a in range(i, i + count)], axis=0)
        q = jnp.concatenate([explicit_pressure(p, e, n, c, a) for a in range(i, i + count)], axis=0)
        return forcing, q

    def step(p, p_next, i, last):
        vertical, pressure = solve(*columns(p, i, 2), wh[...], wl[...])
        for a in range(2):
            rows = slice(a * Y, (a + 1) * Y)
            p_next[i + a + 2, own, :] = pressure[rows]
            if last:
                f[i + a] = vertical[rows] + BUOYANCY * th[i + a]
            else:
                v[i + a] = vertical[rows]

    move_east(p0, e, e, 2, 8)
    move_north(p0, n, n, TOP + 8, TOP + Y - 8)
    for copy in halo0:
        copy.wait()
    move_east(p0, e, e, 0, 2)
    move_east(p0, e, e, 8, 10)
    edges_north(p0, n, n)
    halo1 = [to_left(p1, 8), to_right(p1, 9), to_down(p1, 10), to_up(p1, 11)]
    step(p0, p1, 0, False)
    halo1[0].start()
    step(p0, p1, 6, False)
    halo1[1].start()
    step(p0, p1, 2, False)
    step(p0, p1, 4, False)
    halo1[2].start()
    halo1[3].start()

    for copy in stage1:
        copy.wait()
    r2[hi] = add(r1, lo_size)
    for copy in stage2:
        copy.start()

    move_east(p1, e, e, 2, 8)
    move_north(p1, n, n, TOP + 8, TOP + Y - 8)
    for copy in halo1:
        copy.wait()
    move_east(p1, e, e, 0, 2)
    move_east(p1, e, e, 8, 10)
    edges_north(p1, n, n)
    halo2 = [to_left(p2, 12), to_right(p2, 13), to_down(p2, 14), to_up(p2, 15)]
    step(p1, p2, 0, True)
    halo2[0].start()
    step(p1, p2, 6, True)
    halo2[1].start()
    step(p1, p2, 2, True)
    step(p1, p2, 4, True)
    halo2[2].start()
    halo2[3].start()

    for copy in stage2:
        copy.wait()
    mean = add(r2, hi_size) * (1.0 / (nx * X * ny * Y))
    pull = jnp.broadcast_to(-BUOYANCY * mean[1:2, :], (8, Z))
    vertical, pressure = solve(pull, zero, wh[...], wl[...])
    vertical, pressure = solve(pull + vertical, pressure, wh[...], wl[...])
    vertical, pressure = solve(pull + vertical, pressure, wh[...], wl[...])
    r3[gy] = jnp.where(
        row == 0, mean, jnp.where(row == 1, vertical, jnp.where(row == 2, pressure, 0.0))
    )
    for copy in stage3:
        copy.start()
    for copy in halo2:
        copy.wait()
    for copy in stage3:
        copy.wait()
    total[...] = add(r3, ny)


def kernel_last(
    p, e, n, f, th, hu, r, wh, wl, total, c_ref,
    e_out, n_out, v_out, p_out, th_out, hu_out, r_out, s_out,
    e_new, n_new, v_new, p_new, sem,
):
    copies = []

    def out(src, dst):
        copy = pltpu.make_async_copy(src, dst, sem.at[len(copies)])
        copy.start()
        copies.append(copy)

    out(r, r_out)
    out(th, th_out)
    out(hu, hu_out)
    c = c_ref[...]
    stats = total[...]
    s_out[...] = stats[0:1, :]
    move_east(p, e, e_new, 0, 10)
    out(e_new.at[1:9], e_out)
    move_north(p, n, n_new, TOP + 8, TOP + Y - 8)
    edges_north(p, n, n_new)
    out(n_new.at[:, TOP : TOP + Y, :], n_out)
    for i in range(0, X, 2):
        forcing = jnp.concatenate([f[i], f[i + 1]], axis=0)
        q = jnp.concatenate(
            [explicit_pressure(p, e_new, n_new, c, a) for a in (i, i + 1)], axis=0
        )
        vertical, pressure = solve(forcing, q, wh[...], wl[...])
        vertical = vertical + stats[1:2, :]
        pressure = pressure + stats[2:3, :]
        for a in range(2):
            v_new[i + a] = vertical[a * Y : (a + 1) * Y]
            p_new[i + a] = pressure[a * Y : (a + 1) * Y]
        out(v_new.at[i : i + 2], v_out.at[i : i + 2])
        out(p_new.at[i : i + 2], p_out.at[i : i + 2])
    for copy in copies:
        copy.wait()


def local(lo_size, nx, ny, e, n, v, p, th, hu, sound_speed, radius, multiplicity, count):
    c = sound_speed.reshape(1, Z)
    radius = radius.reshape(SLOTS, ROWS, Y)
    multiplicity = multiplicity.reshape(SLOTS, ROWS, Y)
    stay = pltpu.with_memory_space_constraint
    hbm = pl.BlockSpec(memory_space=pltpu.HBM)
    vmem = pl.BlockSpec(memory_space=pltpu.VMEM)
    dma = pltpu.SemaphoreType.DMA
    hi_size = nx // lo_size
    peers = lo_size + hi_size + ny - 3
    handed = [
        ((X + 4, Y + 16, Z), F32),
        ((X + 2, Y, Z), F32),
        ((X, Y + 16, Z), F32),
        ((X, Y, Z), F32),
        ((X, Y, Z), F32),
        ((X, Y, Z), F32),
        ((SLOTS, ROWS, Y), F32),
        ((2 * Z, 2 * Z), BF16),
        ((2 * Z, 2 * Z), BF16),
        ((8, Z), F32),
    ]
    state = pl.pallas_call(
        functools.partial(kernel_main, lo_size),
        out_shape=tuple(pltpu.VMEM(s, d) for s, d in handed),
        in_specs=[hbm] * 10,
        out_specs=tuple([vmem] * len(handed)),
        scratch_shapes=[
            pltpu.VMEM((X + 4, Y + 16, Z), F32),
            pltpu.VMEM((X + 4, Y + 16, Z), F32),
            pltpu.VMEM((X, Y, Z), F32),
            pltpu.VMEM((1, Z), F32),
            pltpu.VMEM((SLOTS, ROWS, Y), BF16),
            pltpu.VMEM((CLOUD, X, Y), jnp.int32),
            pltpu.VMEM((CLOUD, X, Y), F32),
            pltpu.VMEM((2 * Z, Z), F32),
            pltpu.VMEM((lo_size, 8, Z), F32),
            pltpu.VMEM((hi_size, 8, Z), F32),
            pltpu.VMEM((ny, 8, Z), F32),
            dma((8,)),
            dma((CHUNKS,)),
            dma((CHUNKS,)),
            dma((16,)),
            dma((16,)),
            dma((peers,)),
            dma((peers,)),
        ],
        compiler_params=pltpu.CompilerParams(
            collective_id=0, has_side_effects=True, vmem_limit_bytes=24 << 20
        ),
        name="condense_and_step",
    )(*(stay(x, pltpu.HBM) for x in (e, n, v, p, th, hu, c, radius, multiplicity, count)))
    grid = jax.ShapeDtypeStruct((X, Y, Z), F32)
    outs = pl.pallas_call(
        kernel_last,
        out_shape=(
            (grid,) * 6
            + (
                jax.ShapeDtypeStruct((SLOTS, ROWS, Y), F32),
                jax.ShapeDtypeStruct((1, Z), F32),
            )
        ),
        in_specs=[vmem] * (len(handed) + 1),
        out_specs=tuple([hbm] * 7 + [vmem]),
        scratch_shapes=[
            pltpu.VMEM((X + 2, Y, Z), F32),
            pltpu.VMEM((X, Y + 16, Z), F32),
            pltpu.VMEM((X, Y, Z), F32),
            pltpu.VMEM((X, Y, Z), F32),
            dma((13,)),
        ],
        compiler_params=pltpu.CompilerParams(vmem_limit_bytes=24 << 20),
        name="last_step",
    )(*state, c)
    return outs[:6] + (outs[6].reshape(SLOTS, CLOUD, X, Y), outs[7].reshape(Z))


def solution(mesh):
    nx, ny = mesh.shape["gx"], mesh.shape["gy"]
    lo_size = 8 if nx % 8 == 0 else 2
    grid = P("gx", "gy", None)
    drops = P(None, None, "gx", "gy")
    return jax.shard_map(
        functools.partial(local, lo_size, nx, ny),
        mesh=mesh,
        in_specs=(grid,) * 6 + (P(), drops, drops, P(None, "gx", "gy")),
        out_specs=(grid,) * 6 + (drops, P()),
        check_vma=False,
    )
```

profile of v0, /device:TPU:32, one launch (start us, length us, event | category | flops | bytes accessed | tf_op | source)
XLA Modules:
  0.0 31.2 jit_solution(12352285039510330168)
XLA Ops:
  0.6 0.0 copy-start
  0.6 27.4 %condense_and_step.1 = (f32[12,144,128]{2,1,0:T(8,128)S(1)}, f32[10,128,128]{2,1,0:T(8,128)S(1)}, f32[8,144,128]{2,1,0:T(8,128)S(1)}, f32[8,128,128]{2,1,0:T(8,1...) custom-call(f32[8,128,128]{2,1,0:T(8,128)} %e_hbm.1, ...), custom_call_target="tpu_custom_call" | custom-call | tf_op jit(solution)/shard_map/condense_and_step/pallas_call | solution.py:414
  28.0 0.0 copy-done
  28.0 3.2 %last_step.1 = (f32[8,128,128]{2,1,0:T(8,128)}, f32[8,128,128]{2,1,0:T(8,128)}, f32[8,128,128]{2,1,0:T(8,128)}, f32[8,128,128]{2,1,0:T(8,128)}, f32[8,128,128]{2...) custom-call(f32[12,144,128]{2,1,0:T(8,128)S(1)} %get-tuple-element.26.p, ...), custom_call_target="tpu_custom_call" | custom-call | tf_op jit(solution)/shard_map/last_step/pallas_call | solution.py:445
Async XLA Ops:
  0.6 27.4 %copy-start = (f32[128]{0:T(128)S(1)}, f32[128]{0:T(128)}, u32[]{:S(2)}) copy-start(f32[128]{0:T(128)} %param.16) | copy-start | bytes 1540
where the time goes:
time: 31.3 us; the launch traced here: 31.2 us
  Pallas kernels  30.5 us (97%)
  between operations  0.66 us (2%)
    pallas_call x1, Pallas kernels, local(): pl.pallas_call(functools.partial(kernel_main, lo_size), out_shape=tuple((...  27.4 us
    pallas_call x1, Pallas kernels, local(): pl.pallas_call(kernel_last, out_shape=(grid,) * 6 + (jax.ShapeDtypeStruct...  3.17 us

commit v1 on v0

v1 whole, which is shorter than its diff:
```python
import functools

import jax
import jax.numpy as jnp
from jax import lax
from jax.experimental import pallas as pl
from jax.experimental.pallas import tpu as pltpu
from jax.sharding import PartitionSpec as P

F32 = jnp.float32
BF16 = jnp.bfloat16
MESH = pl.DeviceIdType.MESH
X, Y, Z = 8, 128, 128
SLOTS, CLOUD, BASE = 64, 8, 32
ROWS = CLOUD * X
CHUNKS = 8
PER = SLOTS // CHUNKS
TOP = 8
SLOPE, GROWTH, FLOOR, MASS, LATENT, BUOYANCY = 0.01, 25.0, 0.0625, 0.0004, 200.0, 0.5


def split(x):
    high = x.astype(BF16)
    return high, (x - high.astype(F32)).astype(BF16)


def mm(a, b):
    return jnp.dot(a, b, preferred_element_type=F32)


def times(x, high, low):
    xh, xl = split(x)
    rows = x.shape[0]
    both = mm(jnp.concatenate([xh, xl], axis=0), high)
    return both[:rows] + (both[rows:] + mm(xh, low))


def solve(forcing, explicit, high, low):
    both = times(jnp.concatenate([forcing, explicit], axis=1), high, low)
    return both[:, :Z], explicit + both[:, Z:]


OWN = slice(TOP, TOP + Y)


def move_east(p, e_in, e_out, planes):
    for a in planes:
        e_out[a] = e_in[a] - 0.5 * (p[a + 2, OWN, :] - p[a, OWN, :])


def move_north(p, n, first, last):
    for i in range(X):
        n[i, first:last, :] = n[i, first:last, :] - 0.5 * (
            p[i + 2, first + 1 : last + 1, :] - p[i + 2, first - 1 : last - 1, :]
        )


def explicit_pressure(p, east, west, n, c, i):
    spread = 0.5 * (
        (east - west) + (n[i, TOP + 1 : TOP + Y + 1, :] - n[i, TOP - 1 : TOP + Y - 1, :])
    )
    return p[i + 2, OWN, :] - c * spread


def edges_north(p, n):
    move_north(p, n, TOP - 1, TOP)
    move_north(p, n, TOP, TOP + 8)
    move_north(p, n, TOP + Y - 8, TOP + Y)
    move_north(p, n, TOP + Y, TOP + Y + 1)


def column_matrix(c):
    k = lax.broadcasted_iota(jnp.int32, (Z, Z), 0)
    j = lax.broadcasted_iota(jnp.int32, (Z, Z), 1)
    here = jnp.broadcast_to(c, (Z, Z))
    above = pltpu.roll(here, Z - 1, 1)
    m = jnp.where(k == j, 1.0 + jnp.where(k < Z - 1, here + above, 0.0), 0.0)
    m = m - jnp.where((j == k + 1) & (j < Z - 1), here, 0.0)
    m = m - jnp.where((j == k - 1) & (k < Z - 1), above, 0.0)
    eye = jnp.where(k == j, 1.0, 0.0)
    return eye, eye - m * (1.0 / 3.0)


def column_tables(inverse, c):
    k = lax.broadcasted_iota(jnp.int32, (Z, Z), 0)
    a = jnp.where(k < Z - 1, inverse, 0.0)
    b = a - pltpu.roll(a, 1, 0)
    left = jnp.concatenate([a, b], axis=0)
    j = lax.broadcasted_iota(jnp.int32, (2 * Z, Z), 1)
    m = jnp.where(j < Z - 1, left, 0.0)
    right = (pltpu.roll(m, 1, 1) - m) * c
    return split(jnp.concatenate([left, right], axis=1))


def far_first(count):
    return sorted(range(1, count), key=lambda d: -min(d, count - d))


def kernel_main(
    lo_size,
    e_hbm, n_hbm, v_hbm, p_hbm, th_hbm, hu_hbm, c_hbm, r_hbm, m_hbm, k_hbm,
    p2, e, n, f, th, hu, r, wh, wl, v_new, p_new, total,
    p0, p1, v, c_ref, m_ref, k_ref, cl, xr, a_ref, r1, r2, r3,
    load_sem, r_sem, m_sem, hs, hr, as_, ar,
):
    gx, gy = lax.axis_index("gx"), lax.axis_index("gy")
    nx, ny = lax.axis_size("gx"), lax.axis_size("gy")
    hi_size = nx // lo_size
    lo, hi = lax.rem(gx, lo_size), gx // lo_size
    right, left = lax.rem(gx + 1, nx), lax.rem(gx + nx - 1, nx)
    up, down = lax.rem(gy + 1, ny), lax.rem(gy + ny - 1, ny)

    barrier = pltpu.get_barrier_semaphore()
    lo_peers = [(hi * lo_size + lax.rem(lo + d, lo_size), gy) for d in far_first(lo_size)]
    hi_peers = [(lax.rem(hi + d, hi_size) * lo_size + lo, gy) for d in far_first(hi_size)]
    gy_peers = [(gx, lax.rem(gy + d, ny)) for d in far_first(ny)]
    everyone = gy_peers + hi_peers + lo_peers + [(left, gy), (right, gy)]
    for who in everyone:
        pl.semaphore_signal(barrier, inc=1, device_id=who, device_id_type=MESH)

    def droplets(q):
        part = pl.ds(q * PER, PER)
        return (
            pltpu.make_async_copy(r_hbm.at[part], r.at[part], r_sem.at[q]),
            pltpu.make_async_copy(m_hbm.at[part], m_ref.at[part], m_sem.at[q]),
        )

    pairs = (
        (c_hbm, c_ref),
        (th_hbm, th),
        (hu_hbm, hu),
        (p_hbm.at[0:2], p0.at[2:4, OWN, :]),
        (p_hbm.at[6:8], p0.at[8:10, OWN, :]),
        (e_hbm.at[0:1], e.at[1:2]),
        (e_hbm.at[7:8], e.at[8:9]),
        (k_hbm, k_ref),
        (p_hbm.at[2:6], p0.at[4:8, OWN, :]),
        (e_hbm.at[1:7], e.at[2:8]),
        (n_hbm, n.at[:, OWN, :]),
        (v_hbm, v),
    )
    loads = [
        pltpu.make_async_copy(src, dst, load_sem.at[at]) for at, (src, dst) in enumerate(pairs)
    ]
    for copy in loads[:8]:
        copy.start()
    for q in range(CHUNKS):
        for copy in droplets(q):
            copy.start()
    for copy in loads[8:]:
        copy.start()

    loads[0].wait()
    c = c_ref[...]
    eye, r0 = column_matrix(c)
    xr[0:Z, :] = eye
    xr[Z:, :] = r0

    def square(_, carry):
        x = xr[...]
        high, low = split(x[Z:])
        product = times(x, high, low)
        xr[0:Z, :] = x[:Z] + product[:Z]
        xr[Z:, :] = product[Z:]
        return carry

    lax.fori_loop(0, 6, square, 0)
    high, low = column_tables(xr[0:Z, :] * (1.0 / 3.0), c)
    wh[...] = high
    wl[...] = low

    loads[1].wait()
    loads[2].wait()
    for i in range(X):
        sat = hu[i] * jnp.exp(-SLOPE * th[i]) - 1.0
        cl[:, i : i + 1, :] = GROWTH * jnp.transpose(sat)[BASE : BASE + CLOUD].reshape(CLOUD, 1, Y)

    for copy in loads[3:7]:
        copy.wait()
    a_ref[0] = e[1] - 0.5 * p0[3, OWN, :]
    a_ref[1] = e[8] + 0.5 * p0[8, OWN, :]

    pl.semaphore_wait(barrier, len(everyone))

    def send(src, dst, at, who):
        return pltpu.make_async_remote_copy(
            src_ref=src,
            dst_ref=dst,
            send_sem=hs.at[at],
            recv_sem=hr.at[at],
            device_id=who,
            device_id_type=MESH,
        )

    def exchange(p, at):
        return [
            send(p.at[2:3, OWN, :], p.at[10:11, OWN, :], at, (left, gy)),
            send(p.at[9:10, OWN, :], p.at[1:2, OWN, :], at + 1, (right, gy)),
            send(p.at[3:4, OWN, :], p.at[11:12, OWN, :], at + 2, (left, gy)),
            send(p.at[8:9, OWN, :], p.at[0:1, OWN, :], at + 3, (right, gy)),
            send(p.at[2:10, TOP : TOP + 8, :], p.at[2:10, TOP + Y :, :], at + 4, (gx, down)),
            send(p.at[2:10, TOP + Y - 8 : TOP + Y, :], p.at[2:10, 0:TOP, :], at + 5, (gx, up)),
        ]

    halo0 = [
        send(p_hbm.at[0:1], p0.at[10:11, OWN, :], 0, (left, gy)),
        send(p_hbm.at[7:8], p0.at[1:2, OWN, :], 1, (right, gy)),
        send(a_ref.at[0:1], e.at[9:10], 2, (left, gy)),
        send(a_ref.at[1:2], e.at[0:1], 3, (right, gy)),
        send(p_hbm.at[:, 0:8, :], p0.at[2:10, TOP + Y :, :], 4, (gx, down)),
        send(p_hbm.at[:, Y - 8 :, :], p0.at[2:10, 0:TOP, :], 5, (gx, up)),
        send(n_hbm.at[:, 0:8, :], n.at[:, TOP + Y :, :], 6, (gx, down)),
        send(n_hbm.at[:, Y - 8 :, :], n.at[:, 0:TOP, :], 7, (gx, up)),
    ]
    for copy in halo0:
        copy.start()
    halo1, halo2 = exchange(p1, 8), exchange(p2, 14)

    loads[7].wait()

    def condense(q, acc):
        for copy in droplets(q):
            copy.wait()
        growth = cl[...].reshape(ROWS, Y)
        count = k_ref[...].reshape(ROWS, Y)
        for s in range(PER):
            slot = q * PER + s
            old = r[slot]
            grown = jnp.maximum(old + growth, FLOOR)
            live = count > slot
            mass = m_ref[slot].astype(F32) * (
                grown * grown * lax.rsqrt(grown) - old * old * lax.rsqrt(old)
            )
            r[slot] = jnp.where(live, grown, 0.0)
            acc = acc + jnp.where(live, mass, 0.0)
        return acc

    acc = lax.fori_loop(0, CHUNKS, condense, jnp.zeros((ROWS, Y), F32))
    cl[...] = (MASS * acc).reshape(CLOUD, X, Y)

    zero = jnp.zeros((8, Z), F32)
    percents, warms = zero, zero
    for i in range(X):
        change = cl[:, i : i + 1, :].reshape(CLOUD, Y)
        added = jnp.transpose(
            jnp.concatenate(
                [jnp.zeros((BASE, Y), F32), change, jnp.zeros((Z - BASE - CLOUD, Y), F32)], axis=0
            )
        )
        wet = hu[i] - added
        warm = th[i] + LATENT * added
        hu[i] = wet
        th[i] = warm
        percent = 100.0 * (wet * jnp.exp(-SLOPE * warm) - 1.0)
        percents = percents + jnp.sum(percent.reshape(Y // 8, 8, Z), axis=0)
        warms = warms + jnp.sum(warm.reshape(Y // 8, 8, Z), axis=0)
    row = lax.broadcasted_iota(jnp.int32, (8, Z), 0)

    def gather(buffer, me, who, at):
        return [
            pltpu.make_async_remote_copy(
                src_ref=buffer.at[me],
                dst_ref=buffer.at[me],
                send_sem=as_.at[at + d],
                recv_sem=ar.at[at + d],
                device_id=peer,
                device_id_type=MESH,
            )
            for d, peer in enumerate(who)
        ]

    def add(buffer, count):
        value = buffer[0]
        for d in range(1, count):
            value = value + buffer[d]
        return value

    stage1 = gather(r1, lo, lo_peers, 0)
    stage2 = gather(r2, hi, hi_peers, len(lo_peers))
    stage3 = gather(r3, gy, gy_peers, len(lo_peers) + len(hi_peers))
    r1[lo] = jnp.where(
        row == 0,
        jnp.sum(percents, axis=0, keepdims=True),
        jnp.where(row == 1, jnp.sum(warms, axis=0, keepdims=True), 0.0),
    )
    for copy in stage1:
        copy.start()

    for copy in loads[8:]:
        copy.wait()

    def planes(p, p_next, which, last):
        forcing = jnp.concatenate([v[a] + BUOYANCY * th[a] for a in which], axis=0)
        q = jnp.concatenate(
            [explicit_pressure(p, e[a + 2], e[a], n, c, a) for a in which], axis=0
        )
        vertical, pressure = solve(forcing, q, wh[...], wl[...])
        for at, a in enumerate(which):
            rows = slice(at * Y, (at + 1) * Y)
            p_next[a + 2, OWN, :] = pressure[rows]
            if last:
                f[a] = vertical[rows] + BUOYANCY * th[a]
            else:
                v[a] = vertical[rows]

    def inside(p, halo):
        move_east(p, e, e, range(2, 8))
        move_north(p, n, TOP + 8, TOP + Y - 8)
        for copy in halo[4:]:
            copy.wait()
        edges_north(p, n)

    inside(p0, halo0)
    planes(p0, p1, (2, 3, 4, 5), False)
    for copy in halo0[:4]:
        copy.wait()
    move_east(p0, e, e, (1, 8))
    e[0] = e[0] - 0.5 * p0[2, OWN, :]
    e[9] = e[9] + 0.5 * p0[9, OWN, :]
    planes(p0, p1, (0, 7), False)
    halo1[0].start()
    halo1[1].start()
    planes(p0, p1, (1, 6), False)
    for copy in halo1[2:]:
        copy.start()

    for copy in stage1:
        copy.wait()
    r2[hi] = add(r1, lo_size)
    for copy in stage2:
        copy.start()

    inside(p1, halo1)
    planes(p1, p2, (2, 3, 4, 5), True)
    for copy in stage2:
        copy.wait()
    r3[gy] = add(r2, hi_size)
    for copy in stage3:
        copy.start()
    for copy in halo1[:4]:
        copy.wait()
    move_east(p1, e, e, (0, 1, 8, 9))
    planes(p1, p2, (0, 7), True)
    halo2[0].start()
    halo2[1].start()
    planes(p1, p2, (1, 6), True)
    for copy in halo2[2:]:
        copy.start()

    for copy in stage3:
        copy.wait()
    mean = add(r3, ny) * (1.0 / (nx * X * ny * Y))
    pull = jnp.broadcast_to(-BUOYANCY * mean[1:2, :], (16, Z))
    vertical, pressure = solve(pull, jnp.zeros((16, Z), F32), wh[...], wl[...])
    vertical, pressure = solve(pull + vertical, pressure, wh[...], wl[...])
    vertical, pressure = solve(pull + vertical, pressure, wh[...], wl[...])
    total[...] = jnp.where(row == 0, mean, jnp.where(row == 1, vertical[:8], pressure[:8]))

    inside(p2, halo2)
    which = (2, 3, 4, 5)
    forcing = jnp.concatenate([f[a] for a in which], axis=0)
    q = jnp.concatenate([explicit_pressure(p2, e[a + 2], e[a], n, c, a) for a in which], axis=0)
    inner_v, inner_p = solve(forcing, q, wh[...], wl[...])
    v_new[...] = (inner_v + vertical[0:1]).reshape(4, Y, Z)
    p_new[...] = (inner_p + pressure[0:1]).reshape(4, Y, Z)
    for copy in halo2[:4]:
        copy.wait()


def kernel_last(
    p, e, n, f, th, hu, r, wh, wl, v_in, p_in, total, c_ref,
    e_out, n_out, v_out, p_out, th_out, hu_out, r_out, s_out,
    e_new, v_new, p_new, sem,
):
    copies = []

    def out(src, dst):
        copy = pltpu.make_async_copy(src, dst, sem.at[len(copies)])
        copy.start()
        copies.append(copy)

    out(r, r_out)
    out(th, th_out)
    out(hu, hu_out)
    out(n.at[:, OWN, :], n_out)
    out(e.at[2:8], e_out.at[1:7])
    out(v_in, v_out.at[2:6])
    out(p_in, p_out.at[2:6])
    c = c_ref[...]
    stats = total[...]
    s_out[...] = stats[0:1, :]
    for at, a in enumerate((0, 1, 8, 9)):
        e_new[at] = e[a] - 0.5 * (p[a + 2, OWN, :] - p[a, OWN, :])
    out(e_new.at[1:2], e_out.at[0:1])
    out(e_new.at[2:3], e_out.at[7:8])
    forcing = jnp.concatenate([f[0], f[1], f[6], f[7]], axis=0)
    q = jnp.concatenate(
        [
            explicit_pressure(p, e[2], e_new[0], n, c, 0),
            explicit_pressure(p, e[3], e_new[1], n, c, 1),
            explicit_pressure(p, e_new[2], e[6], n, c, 6),
            explicit_pressure(p, e_new[3], e[7], n, c, 7),
        ],
        axis=0,
    )
    vertical, pressure = solve(forcing, q, wh[...], wl[...])
    v_new[...] = (vertical + stats[1:2, :]).reshape(4, Y, Z)
    p_new[...] = (pressure + stats[2:3, :]).reshape(4, Y, Z)
    out(v_new.at[0:2], v_out.at[0:2])
    out(p_new.at[0:2], p_out.at[0:2])
    out(v_new.at[2:4], v_out.at[6:8])
    out(p_new.at[2:4], p_out.at[6:8])
    for copy in copies:
        copy.wait()


def local(lo_size, nx, ny, e, n, v, p, th, hu, sound_speed, radius, multiplicity, count):
    c = sound_speed.reshape(1, Z)
    radius = radius.reshape(SLOTS, ROWS, Y)
    multiplicity = multiplicity.reshape(SLOTS, ROWS, Y)
    stay = pltpu.with_memory_space_constraint
    hbm = pl.BlockSpec(memory_space=pltpu.HBM)
    vmem = pl.BlockSpec(memory_space=pltpu.VMEM)
    dma = pltpu.SemaphoreType.DMA
    hi_size = nx // lo_size
    peers = lo_size + hi_size + ny - 3
    handed = [
        ((X + 4, Y + 16, Z), F32),
        ((X + 2, Y, Z), F32),
        ((X, Y + 16, Z), F32),
        ((X, Y, Z), F32),
        ((X, Y, Z), F32),
        ((X, Y, Z), F32),
        ((SLOTS, ROWS, Y), F32),
        ((2 * Z, 2 * Z), BF16),
        ((2 * Z, 2 * Z), BF16),
        ((4, Y, Z), F32),
        ((4, Y, Z), F32),
        ((8, Z), F32),
    ]
    state = pl.pallas_call(
        functools.partial(kernel_main, lo_size),
        out_shape=tuple(pltpu.VMEM(s, d) for s, d in handed),
        in_specs=[hbm] * 10,
        out_specs=tuple([vmem] * len(handed)),
        scratch_shapes=[
            pltpu.VMEM((X + 4, Y + 16, Z), F32),
            pltpu.VMEM((X + 4, Y + 16, Z), F32),
            pltpu.VMEM((X, Y, Z), F32),
            pltpu.VMEM((1, Z), F32),
            pltpu.VMEM((SLOTS, ROWS, Y), BF16),
            pltpu.VMEM((CLOUD, X, Y), jnp.int32),
            pltpu.VMEM((CLOUD, X, Y), F32),
            pltpu.VMEM((2 * Z, Z), F32),
            pltpu.VMEM((2, Y, Z), F32),
            pltpu.VMEM((lo_size, 8, Z), F32),
            pltpu.VMEM((hi_size, 8, Z), F32),
            pltpu.VMEM((ny, 8, Z), F32),
            dma((12,)),
            dma((CHUNKS,)),
            dma((CHUNKS,)),
            dma((20,)),
            dma((20,)),
            dma((peers,)),
            dma((peers,)),
        ],
        compiler_params=pltpu.CompilerParams(
            collective_id=0, has_side_effects=True, vmem_limit_bytes=24 << 20
        ),
        name="condense_and_step",
    )(*(stay(x, pltpu.HBM) for x in (e, n, v, p, th, hu, c, radius, multiplicity, count)))
    grid = jax.ShapeDtypeStruct((X, Y, Z), F32)
    outs = pl.pallas_call(
        kernel_last,
        out_shape=(
            (grid,) * 6
            + (
                jax.ShapeDtypeStruct((SLOTS, ROWS, Y), F32),
                jax.ShapeDtypeStruct((1, Z), F32),
            )
        ),
        in_specs=[vmem] * (len(handed) + 1),
        out_specs=tuple([hbm] * 7 + [vmem]),
        scratch_shapes=[
            pltpu.VMEM((4, Y, Z), F32),
            pltpu.VMEM((4, Y, Z), F32),
            pltpu.VMEM((4, Y, Z), F32),
            dma((13,)),
        ],
        compiler_params=pltpu.CompilerParams(vmem_limit_bytes=24 << 20),
        name="last_step",
    )(*state, c)
    return outs[:6] + (outs[6].reshape(SLOTS, CLOUD, X, Y), outs[7].reshape(Z))


def solution(mesh):
    nx, ny = mesh.shape["gx"], mesh.shape["gy"]
    lo_size = 8 if nx % 8 == 0 else 2
    grid = P("gx", "gy", None)
    drops = P(None, None, "gx", "gy")
    return jax.shard_map(
        functools.partial(local, lo_size, nx, ny),
        mesh=mesh,
        in_specs=(grid,) * 6 + (P(), drops, drops, P(None, "gx", "gy")),
        out_specs=(grid,) * 6 + (drops, P()),
        check_vma=False,
    )
```

time: 31.3 us -> 29.8 us (0.952)
  Pallas kernels: 30.5 us -> 29 us
    pallas_call x1, Pallas kernels: 27.4 us -> 25.9 us  [local(): pl.pallas_call(functools.partial(kernel_main, lo_size), out_shape=tuple((...]
where the time goes in v1:
time: 29.8 us; the launch traced here: 29.7 us
  Pallas kernels  29 us (97%)
  between operations  0.66 us (2%)
    pallas_call x1, Pallas kernels, local(): pl.pallas_call(functools.partial(kernel_main, lo_size), out_shape=tuple((...  25.9 us
    pallas_call x1, Pallas kernels, local(): pl.pallas_call(kernel_last, out_shape=(grid,) * 6 + (jax.ShapeDtypeStruct...  3.07 us

profile of v1, /device:TPU:32, one launch (start us, length us, event | category | flops | bytes accessed | tf_op | source)
XLA Modules:
  0.0 29.7 jit_solution(3873387798836809289)
XLA Ops:
  0.6 0.0 copy-start
  0.6 25.9 %condense_and_step.1 = (f32[12,144,128]{2,1,0:T(8,128)S(1)}, f32[10,128,128]{2,1,0:T(8,128)S(1)}, f32[8,144,128]{2,1,0:T(8,128)S(1)}, f32[8,128,128]{2,1,0:T(8,1...) custom-call(f32[8,128,128]{2,1,0:T(8,128)} %e_hbm.1, ...), custom_call_target="tpu_custom_call" | custom-call | tf_op jit(solution)/shard_map/condense_and_step/pallas_call | solution.py:441
  26.6 0.0 copy-done
  26.6 3.1 %last_step.1 = (f32[8,128,128]{2,1,0:T(8,128)}, f32[8,128,128]{2,1,0:T(8,128)}, f32[8,128,128]{2,1,0:T(8,128)}, f32[8,128,128]{2,1,0:T(8,128)}, f32[8,128,128]{2...) custom-call(f32[12,144,128]{2,1,0:T(8,128)S(1)} %get-tuple-element.28.p, ...), custom_call_target="tpu_custom_call" | custom-call | tf_op jit(solution)/shard_map/last_step/pallas_call | solution.py:473
Async XLA Ops:
  0.6 26.0 %copy-start = (f32[128]{0:T(128)S(1)}, f32[128]{0:T(128)}, u32[]{:S(2)}) copy-start(f32[128]{0:T(128)} %param.16) | copy-start | bytes 1540

commit v2 on v1

--- a/solution.py
+++ b/solution.py
@@ -96,12 +96,17 @@
     return sorted(range(1, count), key=lambda d: -min(d, count - d))
 
 
+def row_order(nh, ny):
+    steps = [(h, y, c) for h in range(nh) for y in range(ny) for c in range(2)][1:]
+    return sorted(steps, key=lambda t: -(min(t[0], nh - t[0]) + min(t[1], ny - t[1])) * 2 - t[2])
+
+
 def kernel_main(
     lo_size,
     e_hbm, n_hbm, v_hbm, p_hbm, th_hbm, hu_hbm, c_hbm, r_hbm, m_hbm, k_hbm,
     p2, e, n, f, th, hu, r, wh, wl, v_new, p_new, total,
-    p0, p1, v, c_ref, m_ref, k_ref, cl, xr, a_ref, r1, r2, r3,
-    load_sem, r_sem, m_sem, hs, hr, as_, ar,
+    p0, p1, v, c_ref, m_ref, k_ref, cl, xr, a_ref, r1, r3,
+    load_sem, r_sem, m_sem, hs, hr, as_, ar, x_sem, z_sem,
 ):
     gx, gy = lax.axis_index("gx"), lax.axis_index("gy")
     nx, ny = lax.axis_size("gx"), lax.axis_size("gy")
@@ -111,12 +116,24 @@
     up, down = lax.rem(gy + 1, ny), lax.rem(gy + ny - 1, ny)
 
     barrier = pltpu.get_barrier_semaphore()
-    lo_peers = [(hi * lo_size + lax.rem(lo + d, lo_size), gy) for d in far_first(lo_size)]
-    hi_peers = [(lax.rem(hi + d, hi_size) * lo_size + lo, gy) for d in far_first(hi_size)]
+    lo_peers = [(hi * lo_size + lax.rem(lo + d, lo_size), gy) for d in range(1, lo_size)]
+    hi_peers = [(lax.rem(hi + d, hi_size) * lo_size + lo, gy) for d in range(1, hi_size)]
     gy_peers = [(gx, lax.rem(gy + d, ny)) for d in far_first(ny)]
-    everyone = gy_peers + hi_peers + lo_peers + [(left, gy), (right, gy)]
+    relay = ny == 8
+    gy_near = [(gx, lax.rem(gy + d, ny)) for d in (1, 2, 6, 7)] if relay else gy_peers
+    gy_two = [(gx, lax.rem(gy + d, ny)) for d in (2, 6)] if relay else []
+    everyone = gy_near + hi_peers + lo_peers + [(left, gy), (right, gy)]
     for who in everyone:
         pl.semaphore_signal(barrier, inc=1, device_id=who, device_id_type=MESH)
+    row_peers = [
+        (
+            lax.rem(hi + dh, hi_size) * lo_size
+            + lax.rem(lo // 2 + dy, lo_size // 2) * 2
+            + lax.rem(lo + dc, 2),
+            gy,
+        )
+        for dh, dy, dc in row_order(hi_size, lo_size // 2)
+    ]
 
     def droplets(q):
         part = pl.ds(q * PER, PER)
@@ -214,6 +231,10 @@
     ]
     for copy in halo0:
         copy.start()
+    for who in hi_peers:
+        pl.semaphore_signal(x_sem, inc=1, device_id=who, device_id_type=MESH)
+    for who in gy_two:
+        pl.semaphore_signal(z_sem, inc=1, device_id=who, device_id_type=MESH)
     halo1, halo2 = exchange(p1, 8), exchange(p2, 14)
 
     loads[7].wait()
@@ -275,14 +296,14 @@
             value = value + buffer[d]
         return value
 
-    stage1 = gather(r1, lo, lo_peers, 0)
-    stage2 = gather(r2, hi, hi_peers, len(lo_peers))
-    stage3 = gather(r3, gy, gy_peers, len(lo_peers) + len(hi_peers))
-    r1[lo] = jnp.where(
+    stage1 = gather(r1, gx, row_peers, 0)
+    stage2 = gather(r3, gy, gy_peers, len(row_peers))
+    r1[gx] = jnp.where(
         row == 0,
         jnp.sum(percents, axis=0, keepdims=True),
         jnp.where(row == 1, jnp.sum(warms, axis=0, keepdims=True), 0.0),
     )
+    pl.semaphore_wait(x_sem, len(hi_peers))
     for copy in stage1:
         copy.start()
 
@@ -303,14 +324,17 @@
             else:
                 v[a] = vertical[rows]
 
-    def inside(p, halo):
+    def inside(p):
         move_east(p, e, e, range(2, 8))
         move_north(p, n, TOP + 8, TOP + Y - 8)
+
+    def north_edges(p, halo):
         for copy in halo[4:]:
             copy.wait()
         edges_north(p, n)
 
-    inside(p0, halo0)
+    inside(p0)
+    north_edges(p0, halo0)
     planes(p0, p1, (2, 3, 4, 5), False)
     for copy in halo0[:4]:
         copy.wait()
@@ -324,19 +348,16 @@
     for copy in halo1[2:]:
         copy.start()
 
+    inside(p1)
     for copy in stage1:
         copy.wait()
-    r2[hi] = add(r1, lo_size)
+    r3[gy] = add(r1, nx)
+    if relay:
+        pl.semaphore_wait(z_sem, len(gy_two))
     for copy in stage2:
         copy.start()
-
-    inside(p1, halo1)
+    north_edges(p1, halo1)
     planes(p1, p2, (2, 3, 4, 5), True)
-    for copy in stage2:
-        copy.wait()
-    r3[gy] = add(r2, hi_size)
-    for copy in stage3:
-        copy.start()
     for copy in halo1[:4]:
         copy.wait()
     move_east(p1, e, e, (0, 1, 8, 9))
@@ -347,7 +368,8 @@
     for copy in halo2[2:]:
         copy.start()
 
-    for copy in stage3:
+    inside(p2)
+    for copy in stage2:
         copy.wait()
     mean = add(r3, ny) * (1.0 / (nx * X * ny * Y))
     pull = jnp.broadcast_to(-BUOYANCY * mean[1:2, :], (16, Z))
@@ -356,7 +378,7 @@
     vertical, pressure = solve(pull + vertical, pressure, wh[...], wl[...])
     total[...] = jnp.where(row == 0, mean, jnp.where(row == 1, vertical[:8], pressure[:8]))
 
-    inside(p2, halo2)
+    north_edges(p2, halo2)
     which = (2, 3, 4, 5)
     forcing = jnp.concatenate([f[a] for a in which], axis=0)
     q = jnp.concatenate([explicit_pressure(p2, e[a + 2], e[a], n, c, a) for a in which], axis=0)
@@ -422,8 +444,7 @@
     hbm = pl.BlockSpec(memory_space=pltpu.HBM)
     vmem = pl.BlockSpec(memory_space=pltpu.VMEM)
     dma = pltpu.SemaphoreType.DMA
-    hi_size = nx // lo_size
-    peers = lo_size + hi_size + ny - 3
+    peers = nx + ny - 2
     handed = [
         ((X + 4, Y + 16, Z), F32),
         ((X + 2, Y, Z), F32),
@@ -453,8 +474,7 @@
             pltpu.VMEM((CLOUD, X, Y), F32),
             pltpu.VMEM((2 * Z, Z), F32),
             pltpu.VMEM((2, Y, Z), F32),
-            pltpu.VMEM((lo_size, 8, Z), F32),
-            pltpu.VMEM((hi_size, 8, Z), F32),
+            pltpu.VMEM((nx, 8, Z), F32),
             pltpu.VMEM((ny, 8, Z), F32),
             dma((12,)),
             dma((CHUNKS,)),
@@ -463,6 +483,8 @@
             dma((20,)),
             dma((peers,)),
             dma((peers,)),
+            pltpu.SemaphoreType.REGULAR,
+            pltpu.SemaphoreType.REGULAR,
         ],
         compiler_params=pltpu.CompilerParams(
             collective_id=0, has_side_effects=True, vmem_limit_bytes=24 << 20

time: 29.8 us -> 29.4 us (0.987)
  Pallas kernels: 29 us -> 28.7 us
    pallas_call x1, Pallas kernels: 25.9 us -> 25.6 us  [local(): pl.pallas_call(functools.partial(kernel_main, lo_size), out_shape=tuple((...]
where the time goes in v2:
time: 29.4 us; the launch traced here: 29.3 us
  Pallas kernels  28.7 us (98%)
  between operations  0.66 us (2%)
    pallas_call x1, Pallas kernels, local(): pl.pallas_call(functools.partial(kernel_main, lo_size), out_shape=tuple((...  25.6 us
    pallas_call x1, Pallas kernels, local(): pl.pallas_call(kernel_last, out_shape=(grid,) * 6 + (jax.ShapeDtypeStruct...  3.07 us

profile of v2, /device:TPU:32, one launch (start us, length us, event | category | flops | bytes accessed | tf_op | source)
XLA Modules:
  0.0 29.3 jit_solution(9050100917366724719)
XLA Ops:
  0.6 0.0 copy-start
  0.6 25.6 %condense_and_step.1 = (f32[12,144,128]{2,1,0:T(8,128)S(1)}, f32[10,128,128]{2,1,0:T(8,128)S(1)}, f32[8,144,128]{2,1,0:T(8,128)S(1)}, f32[8,128,128]{2,1,0:T(8,1...) custom-call(f32[8,128,128]{2,1,0:T(8,128)} %e_hbm.1, ...), custom_call_target="tpu_custom_call" | custom-call | tf_op jit(solution)/shard_map/condense_and_step/pallas_call | solution.py:462
  26.2 0.0 copy-done
  26.2 3.1 %last_step.1 = (f32[8,128,128]{2,1,0:T(8,128)}, f32[8,128,128]{2,1,0:T(8,128)}, f32[8,128,128]{2,1,0:T(8,128)}, f32[8,128,128]{2,1,0:T(8,128)}, f32[8,128,128]{2...) custom-call(f32[12,144,128]{2,1,0:T(8,128)S(1)} %get-tuple-element.28.p, ...), custom_call_target="tpu_custom_call" | custom-call | tf_op jit(solution)/shard_map/last_step/pallas_call | solution.py:495
Async XLA Ops:
  0.6 25.6 %copy-start = (f32[128]{0:T(128)S(1)}, f32[128]{0:T(128)}, u32[]{:S(2)}) copy-start(f32[128]{0:T(128)} %param.16) | copy-start | bytes 1540

commit v3 on v1

--- a/solution.py
+++ b/solution.py
@@ -13,7 +13,7 @@
 X, Y, Z = 8, 128, 128
 SLOTS, CLOUD, BASE = 64, 8, 32
 ROWS = CLOUD * X
-CHUNKS = 8
+CHUNKS = 4
 PER = SLOTS // CHUNKS
 TOP = 8
 SLOPE, GROWTH, FLOOR, MASS, LATENT, BUOYANCY = 0.01, 25.0, 0.0625, 0.0004, 200.0, 0.5
@@ -78,7 +78,7 @@
     m = m - jnp.where((j == k + 1) & (j < Z - 1), here, 0.0)
     m = m - jnp.where((j == k - 1) & (k < Z - 1), above, 0.0)
     eye = jnp.where(k == j, 1.0, 0.0)
-    return eye, eye - m * (1.0 / 3.0)
+    return eye, m
 
 
 def column_tables(inverse, c):
@@ -100,8 +100,8 @@
     lo_size,
     e_hbm, n_hbm, v_hbm, p_hbm, th_hbm, hu_hbm, c_hbm, r_hbm, m_hbm, k_hbm,
     p2, e, n, f, th, hu, r, wh, wl, v_new, p_new, total,
-    p0, p1, v, c_ref, m_ref, k_ref, cl, xr, a_ref, r1, r2, r3,
-    load_sem, r_sem, m_sem, hs, hr, as_, ar,
+    p0, p1, v, c_ref, m_ref, k_ref, cl, xr, a_ref, alone, spill, th_high, th_low, r1, r2, r3,
+    load_sem, r_sem, m_sem, hs, hr, as_, ar, z_sem,
 ):
     gx, gy = lax.axis_index("gx"), lax.axis_index("gy")
     nx, ny = lax.axis_size("gx"), lax.axis_size("gy")
@@ -114,10 +114,12 @@
     lo_peers = [(hi * lo_size + lax.rem(lo + d, lo_size), gy) for d in far_first(lo_size)]
     hi_peers = [(lax.rem(hi + d, hi_size) * lo_size + lo, gy) for d in far_first(hi_size)]
     gy_peers = [(gx, lax.rem(gy + d, ny)) for d in far_first(ny)]
-    everyone = gy_peers + hi_peers + lo_peers + [(left, gy), (right, gy)]
+    relay = ny == 8
+    gy_near = [(gx, lax.rem(gy + d, ny)) for d in (1, 2, 6, 7)] if relay else gy_peers
+    gy_two = [(gx, lax.rem(gy + d, ny)) for d in (2, 6)] if relay else []
+    everyone = gy_near + hi_peers + lo_peers + [(left, gy), (right, gy)]
     for who in everyone:
         pl.semaphore_signal(barrier, inc=1, device_id=who, device_id_type=MESH)
-
     def droplets(q):
         part = pl.ds(q * PER, PER)
         return (
@@ -129,32 +131,32 @@
         (c_hbm, c_ref),
         (th_hbm, th),
         (hu_hbm, hu),
-        (p_hbm.at[0:2], p0.at[2:4, OWN, :]),
-        (p_hbm.at[6:8], p0.at[8:10, OWN, :]),
-        (e_hbm.at[0:1], e.at[1:2]),
-        (e_hbm.at[7:8], e.at[8:9]),
         (k_hbm, k_ref),
-        (p_hbm.at[2:6], p0.at[4:8, OWN, :]),
-        (e_hbm.at[1:7], e.at[2:8]),
+        (p_hbm, p0.at[2:10, OWN, :]),
+        (e_hbm, e.at[1:9]),
         (n_hbm, n.at[:, OWN, :]),
         (v_hbm, v),
     )
     loads = [
         pltpu.make_async_copy(src, dst, load_sem.at[at]) for at, (src, dst) in enumerate(pairs)
     ]
-    for copy in loads[:8]:
+    for copy in loads[:4]:
         copy.start()
     for q in range(CHUNKS):
         for copy in droplets(q):
             copy.start()
-    for copy in loads[8:]:
+        if q == 0:
+            for copy in loads[4:6]:
+                copy.start()
+    for copy in loads[6:]:
         copy.start()
 
     loads[0].wait()
     c = c_ref[...]
-    eye, r0 = column_matrix(c)
-    xr[0:Z, :] = eye
-    xr[Z:, :] = r0
+    eye, m = column_matrix(c)
+    half = 0.5 * (3.0 * eye - m)
+    xr[0:Z, :] = (6.0 * eye - m) * (1.0 / 7.0)
+    xr[Z:, :] = (2.0 * times(half, *split(half)) - eye) * (2.0 / 7.0)
 
     def square(_, carry):
         x = xr[...]
@@ -164,8 +166,8 @@
         xr[Z:, :] = product[Z:]
         return carry
 
-    lax.fori_loop(0, 6, square, 0)
-    high, low = column_tables(xr[0:Z, :] * (1.0 / 3.0), c)
+    lax.fori_loop(0, 4, square, 0)
+    high, low = column_tables(xr[0:Z, :], c)
     wh[...] = high
     wl[...] = low
 
@@ -175,7 +177,7 @@
         sat = hu[i] * jnp.exp(-SLOPE * th[i]) - 1.0
         cl[:, i : i + 1, :] = GROWTH * jnp.transpose(sat)[BASE : BASE + CLOUD].reshape(CLOUD, 1, Y)
 
-    for copy in loads[3:7]:
+    for copy in loads[4:6]:
         copy.wait()
     a_ref[0] = e[1] - 0.5 * p0[3, OWN, :]
     a_ref[1] = e[8] + 0.5 * p0[8, OWN, :]
@@ -192,12 +194,12 @@
             device_id_type=MESH,
         )
 
-    def exchange(p, at):
+    def exchange(p, outer, at):
         return [
-            send(p.at[2:3, OWN, :], p.at[10:11, OWN, :], at, (left, gy)),
-            send(p.at[9:10, OWN, :], p.at[1:2, OWN, :], at + 1, (right, gy)),
-            send(p.at[3:4, OWN, :], p.at[11:12, OWN, :], at + 2, (left, gy)),
-            send(p.at[8:9, OWN, :], p.at[0:1, OWN, :], at + 3, (right, gy)),
+            send(outer[0], p.at[10:11, OWN, :], at, (left, gy)),
+            send(outer[1], p.at[1:2, OWN, :], at + 1, (right, gy)),
+            send(outer[2], p.at[11:12, OWN, :], at + 2, (left, gy)),
+            send(outer[3], p.at[0:1, OWN, :], at + 3, (right, gy)),
             send(p.at[2:10, TOP : TOP + 8, :], p.at[2:10, TOP + Y :, :], at + 4, (gx, down)),
             send(p.at[2:10, TOP + Y - 8 : TOP + Y, :], p.at[2:10, 0:TOP, :], at + 5, (gx, up)),
         ]
@@ -212,11 +214,14 @@
         send(n_hbm.at[:, 0:8, :], n.at[:, TOP + Y :, :], 6, (gx, down)),
         send(n_hbm.at[:, Y - 8 :, :], n.at[:, 0:TOP, :], 7, (gx, up)),
     ]
-    for copy in halo0:
-        copy.start()
-    halo1, halo2 = exchange(p1, 8), exchange(p2, 14)
-
-    loads[7].wait()
+    for copy in halo0[:2] + halo0[4:] + halo0[2:4]:
+        copy.start()
+    for who in gy_two:
+        pl.semaphore_signal(z_sem, inc=1, device_id=who, device_id_type=MESH)
+    halo1 = exchange(p1, [alone.at[i : i + 1] for i in range(4)], 8)
+    halo2 = exchange(p2, [p2.at[a : a + 1, OWN, :] for a in (2, 9, 3, 8)], 14)
+
+    loads[3].wait()
 
     def condense(q, acc):
         for copy in droplets(q):
@@ -286,7 +291,7 @@
     for copy in stage1:
         copy.start()
 
-    for copy in loads[8:]:
+    for copy in loads[6:]:
         copy.wait()
 
     def planes(p, p_next, which, last):
@@ -303,26 +308,67 @@
             else:
                 v[a] = vertical[rows]
 
-    def inside(p, halo):
+    def inside(p):
         move_east(p, e, e, range(2, 8))
         move_north(p, n, TOP + 8, TOP + Y - 8)
+
+    def north_edges(p, halo):
         for copy in halo[4:]:
             copy.wait()
         edges_north(p, n)
 
-    inside(p0, halo0)
+    inside(p0)
+    north_edges(p0, halo0)
+    e[1] = e[1] - 0.5 * p0[3, OWN, :]
+    e[8] = e[8] + 0.5 * p0[8, OWN, :]
+
+    def by_itself(which, at):
+        forcing = jnp.concatenate([v[a] + BUOYANCY * th[a] for a in which], axis=0)
+        q = []
+        for a in which:
+            west = -0.5 * p0[2, OWN, :] if a == 0 else e[a]
+            east = 0.5 * p0[9, OWN, :] if a == 7 else e[a + 2]
+            q.append(explicit_pressure(p0, east, west, n, c, a))
+        vertical, pressure = solve(forcing, jnp.concatenate(q, axis=0), wh[...], wl[...])
+        for i, a in enumerate(which):
+            v[a] = vertical[i * Y : (i + 1) * Y]
+            alone[at + i] = pressure[i * Y : (i + 1) * Y]
+            halo1[at + i].start()
+
+    by_itself((0, 7), 0)
+    by_itself((1, 6), 2)
     planes(p0, p1, (2, 3, 4, 5), False)
+
+    def added_pressure(planes_of_q):
+        q = jnp.concatenate(planes_of_q, axis=0)
+        both = times(q, wh[Z:, :], wl[Z:, :])
+        return both[:, :Z], q + both[:, Z:]
+
+    quarter, half_c = 0.25 * c, 0.5 * c
+    _, pressure = added_pressure(
+        [
+            quarter * p0[2, OWN, :],
+            -half_c * a_ref[0],
+            half_c * a_ref[1],
+            quarter * p0[9, OWN, :],
+        ]
+    )
+    spill[...] = pressure.reshape(4, Y, Z)
+
     for copy in halo0[:4]:
         copy.wait()
-    move_east(p0, e, e, (1, 8))
+    vertical, pressure = added_pressure(
+        [half_c * e[0], -half_c * e[9], quarter * p0[1, OWN, :], quarter * p0[10, OWN, :]]
+    )
+    for i, a in enumerate((0, 7, 1, 6)):
+        v[a] = v[a] + vertical[i * Y : (i + 1) * Y]
+        p1[a + 2, OWN, :] = alone[i] + pressure[i * Y : (i + 1) * Y]
+    halo1[4].start()
+    halo1[5].start()
     e[0] = e[0] - 0.5 * p0[2, OWN, :]
+    e[1] = e[1] + 0.5 * p0[1, OWN, :]
+    e[8] = e[8] - 0.5 * p0[10, OWN, :]
     e[9] = e[9] + 0.5 * p0[9, OWN, :]
-    planes(p0, p1, (0, 7), False)
-    halo1[0].start()
-    halo1[1].start()
-    planes(p0, p1, (1, 6), False)
-    for copy in halo1[2:]:
-        copy.start()
 
     for copy in stage1:
         copy.wait()
@@ -330,39 +376,55 @@
     for copy in stage2:
         copy.start()
 
-    inside(p1, halo1)
-    planes(p1, p2, (2, 3, 4, 5), True)
-    for copy in stage2:
-        copy.wait()
-    r3[gy] = add(r2, hi_size)
-    for copy in stage3:
-        copy.start()
+    eye_v, eye_p = solve(eye, jnp.zeros((Z, Z), F32), wh[...], wl[...])
+    eye_v, eye_p = solve(eye + eye_v, eye_p, wh[...], wl[...])
+    eye_v, eye_p = solve(eye + eye_v, eye_p, wh[...], wl[...])
+    high, low = split(-BUOYANCY * jnp.concatenate([eye_v, eye_p], axis=1))
+    th_high[...] = high
+    th_low[...] = low
+
+    inside(p1)
+    north_edges(p1, halo1)
     for copy in halo1[:4]:
         copy.wait()
-    move_east(p1, e, e, (0, 1, 8, 9))
+    e[0] = e[0] - 0.5 * (p1[2, OWN, :] - (p1[0, OWN, :] + spill[0]))
+    e[1] = e[1] - 0.5 * (p1[3, OWN, :] - (p1[1, OWN, :] + spill[1]))
+    e[8] = e[8] - 0.5 * ((p1[10, OWN, :] + spill[2]) - p1[8, OWN, :])
+    e[9] = e[9] - 0.5 * ((p1[11, OWN, :] + spill[3]) - p1[9, OWN, :])
     planes(p1, p2, (0, 7), True)
     halo2[0].start()
     halo2[1].start()
     planes(p1, p2, (1, 6), True)
-    for copy in halo2[2:]:
-        copy.start()
-
+    for copy in halo2[2:4]:
+        copy.start()
+
+    for copy in stage2:
+        copy.wait()
+    r3[gy] = add(r2, hi_size)
+    if relay:
+        pl.semaphore_wait(z_sem, len(gy_two))
     for copy in stage3:
-        copy.wait()
-    mean = add(r3, ny) * (1.0 / (nx * X * ny * Y))
-    pull = jnp.broadcast_to(-BUOYANCY * mean[1:2, :], (16, Z))
-    vertical, pressure = solve(pull, jnp.zeros((16, Z), F32), wh[...], wl[...])
-    vertical, pressure = solve(pull + vertical, pressure, wh[...], wl[...])
-    vertical, pressure = solve(pull + vertical, pressure, wh[...], wl[...])
-    total[...] = jnp.where(row == 0, mean, jnp.where(row == 1, vertical[:8], pressure[:8]))
-
-    inside(p2, halo2)
+        copy.start()
+    planes(p1, p2, (2, 3, 4, 5), True)
+    for copy in halo2[4:]:
+        copy.start()
+
+    inside(p2)
+    north_edges(p2, halo2)
     which = (2, 3, 4, 5)
     forcing = jnp.concatenate([f[a] for a in which], axis=0)
     q = jnp.concatenate([explicit_pressure(p2, e[a + 2], e[a], n, c, a) for a in which], axis=0)
     inner_v, inner_p = solve(forcing, q, wh[...], wl[...])
-    v_new[...] = (inner_v + vertical[0:1]).reshape(4, Y, Z)
-    p_new[...] = (inner_p + pressure[0:1]).reshape(4, Y, Z)
+    v_new[...] = inner_v.reshape(4, Y, Z)
+    p_new[...] = inner_p.reshape(4, Y, Z)
+
+    for copy in stage3:
+        copy.wait()
+    mean = add(r3, ny) * (1.0 / (nx * X * ny * Y))
+    pull = times(jnp.concatenate([mean, mean], axis=0), th_high[...], th_low[...])[1:2, :]
+    v_new[...] = v_new[...] + pull[:, :Z]
+    p_new[...] = p_new[...] + pull[:, Z:]
+    total[...] = jnp.where(row == 0, mean, jnp.where(row == 1, pull[:, :Z], pull[:, Z:]))
     for copy in halo2[:4]:
         copy.wait()
 
@@ -422,8 +484,7 @@
     hbm = pl.BlockSpec(memory_space=pltpu.HBM)
     vmem = pl.BlockSpec(memory_space=pltpu.VMEM)
     dma = pltpu.SemaphoreType.DMA
-    hi_size = nx // lo_size
-    peers = lo_size + hi_size + ny - 3
+    peers = lo_size + nx // lo_size + ny - 3
     handed = [
         ((X + 4, Y + 16, Z), F32),
         ((X + 2, Y, Z), F32),
@@ -453,16 +514,21 @@
             pltpu.VMEM((CLOUD, X, Y), F32),
             pltpu.VMEM((2 * Z, Z), F32),
             pltpu.VMEM((2, Y, Z), F32),
+            pltpu.VMEM((4, Y, Z), F32),
+            pltpu.VMEM((4, Y, Z), F32),
+            pltpu.VMEM((Z, 2 * Z), BF16),
+            pltpu.VMEM((Z, 2 * Z), BF16),
             pltpu.VMEM((lo_size, 8, Z), F32),
-            pltpu.VMEM((hi_size, 8, Z), F32),
+            pltpu.VMEM((nx // lo_size, 8, Z), F32),
             pltpu.VMEM((ny, 8, Z), F32),
-            dma((12,)),
+            dma((8,)),
             dma((CHUNKS,)),
             dma((CHUNKS,)),
             dma((20,)),
             dma((20,)),
             dma((peers,)),
             dma((peers,)),
+            pltpu.SemaphoreType.REGULAR,
         ],
         compiler_params=pltpu.CompilerParams(
             collective_id=0, has_side_effects=True, vmem_limit_bytes=24 << 20

time: 29.8 us -> 27.7 us (0.930)
  Pallas kernels: 29 us -> 26.8 us
    pallas_call x1, Pallas kernels: 25.9 us -> 23.7 us  [local(): pl.pallas_call(functools.partial(kernel_main, lo_size), out_shape=tuple((...]
where the time goes in v3:
time: 27.7 us; the launch traced here: 27.5 us
  Pallas kernels  26.8 us (97%)
  between operations  0.66 us (2%)
    pallas_call x1, Pallas kernels, local(): pl.pallas_call(functools.partial(kernel_main, lo_size), out_shape=tuple((...  23.7 us
    pallas_call x1, Pallas kernels, local(): pl.pallas_call(kernel_last, out_shape=(grid,) * 6 + (jax.ShapeDtypeStruct...  3.07 us

profile of v3, /device:TPU:32, one launch (start us, length us, event | category | flops | bytes accessed | tf_op | source)
XLA Modules:
  0.0 27.5 jit_solution(5170577474588634609)
XLA Ops:
  0.6 0.0 copy-start
  0.6 23.7 %condense_and_step.1 = (f32[12,144,128]{2,1,0:T(8,128)S(1)}, f32[10,128,128]{2,1,0:T(8,128)S(1)}, f32[8,144,128]{2,1,0:T(8,128)S(1)}, f32[8,128,128]{2,1,0:T(8,1...) custom-call(f32[8,128,128]{2,1,0:T(8,128)} %e_hbm.1, ...), custom_call_target="tpu_custom_call" | custom-call | tf_op jit(solution)/shard_map/condense_and_step/pallas_call | solution.py:502
  24.4 0.0 copy-done
  24.4 3.1 %last_step.1 = (f32[8,128,128]{2,1,0:T(8,128)}, f32[8,128,128]{2,1,0:T(8,128)}, f32[8,128,128]{2,1,0:T(8,128)}, f32[8,128,128]{2,1,0:T(8,128)}, f32[8,128,128]{2...) custom-call(f32[12,144,128]{2,1,0:T(8,128)S(1)} %get-tuple-element.28.p, ...), custom_call_target="tpu_custom_call" | custom-call | tf_op jit(solution)/shard_map/last_step/pallas_call | solution.py:539
Async XLA Ops:
  0.6 23.7 %copy-start = (f32[128]{0:T(128)S(1)}, f32[128]{0:T(128)}, u32[]{:S(2)}) copy-start(f32[128]{0:T(128)} %param.16) | copy-start | bytes 1540

commit v4 on v3

--- a/solution.py
+++ b/solution.py
@@ -55,18 +55,27 @@
         )
 
 
-def explicit_pressure(p, east, west, n, c, i):
-    spread = 0.5 * (
-        (east - west) + (n[i, TOP + 1 : TOP + Y + 1, :] - n[i, TOP - 1 : TOP + Y - 1, :])
-    )
-    return p[i + 2, OWN, :] - c * spread
+def explicit_pressure(p, east, west, n, c, i, first=0, last=Y):
+    low, high = TOP + first, TOP + last
+    spread = 0.5 * ((east - west) + (n[i, low + 1 : high + 1, :] - n[i, low - 1 : high - 1, :]))
+    return p[i + 2, low:high, :] - c * spread
 
 
 def edges_north(p, n):
-    move_north(p, n, TOP - 1, TOP)
-    move_north(p, n, TOP, TOP + 8)
-    move_north(p, n, TOP + Y - 8, TOP + Y)
-    move_north(p, n, TOP + Y, TOP + Y + 1)
+    move_north(p, n, TOP - 1, TOP + 1)
+    move_north(p, n, TOP + Y - 1, TOP + Y + 1)
+
+
+def pack_rows(p, rows):
+    for side, first in enumerate((TOP, TOP + Y - 2)):
+        for i in range(2):
+            rows[side, i] = p[2 : X + 2, first + i : first + i + 1, :].reshape(X, Z)
+
+
+def unpack_rows(rows, p):
+    for side, first in enumerate((TOP + Y, TOP - 2)):
+        for i in range(2):
+            p[2 : X + 2, first + i : first + i + 1, :] = rows[side, i].reshape(X, 1, Z)
 
 
 def column_matrix(c):
@@ -100,7 +109,7 @@
     lo_size,
     e_hbm, n_hbm, v_hbm, p_hbm, th_hbm, hu_hbm, c_hbm, r_hbm, m_hbm, k_hbm,
     p2, e, n, f, th, hu, r, wh, wl, v_new, p_new, total,
-    p0, p1, v, c_ref, m_ref, k_ref, cl, xr, a_ref, alone, spill, th_high, th_low, r1, r2, r3,
+    p0, p1, v, c_ref, m_ref, k_ref, cl, xr, a_ref, alone, spill, rows_out, rows_in, th_high, th_low, r1, r2, r3,
     load_sem, r_sem, m_sem, hs, hr, as_, ar, z_sem,
 ):
     gx, gy = lax.axis_index("gx"), lax.axis_index("gy")
@@ -182,6 +191,7 @@
     a_ref[0] = e[1] - 0.5 * p0[3, OWN, :]
     a_ref[1] = e[8] + 0.5 * p0[8, OWN, :]
 
+    pack_rows(p0, rows_out.at[0])
     pl.semaphore_wait(barrier, len(everyone))
 
     def send(src, dst, at, who):
@@ -194,32 +204,57 @@
             device_id_type=MESH,
         )
 
-    def exchange(p, outer, at):
+    def rows_of(k, at):
+        return [
+            send(rows_out.at[k, 0], rows_in.at[k, 0], at, (gx, down)),
+            send(rows_out.at[k, 1], rows_in.at[k, 1], at + 1, (gx, up)),
+        ]
+
+    def exchange(p, k, outer, at):
         return [
             send(outer[0], p.at[10:11, OWN, :], at, (left, gy)),
             send(outer[1], p.at[1:2, OWN, :], at + 1, (right, gy)),
             send(outer[2], p.at[11:12, OWN, :], at + 2, (left, gy)),
             send(outer[3], p.at[0:1, OWN, :], at + 3, (right, gy)),
-            send(p.at[2:10, TOP : TOP + 8, :], p.at[2:10, TOP + Y :, :], at + 4, (gx, down)),
-            send(p.at[2:10, TOP + Y - 8 : TOP + Y, :], p.at[2:10, 0:TOP, :], at + 5, (gx, up)),
-        ]
+        ] + rows_of(k, at + 4)
 
     halo0 = [
         send(p_hbm.at[0:1], p0.at[10:11, OWN, :], 0, (left, gy)),
         send(p_hbm.at[7:8], p0.at[1:2, OWN, :], 1, (right, gy)),
         send(a_ref.at[0:1], e.at[9:10], 2, (left, gy)),
         send(a_ref.at[1:2], e.at[0:1], 3, (right, gy)),
-        send(p_hbm.at[:, 0:8, :], p0.at[2:10, TOP + Y :, :], 4, (gx, down)),
-        send(p_hbm.at[:, Y - 8 :, :], p0.at[2:10, 0:TOP, :], 5, (gx, up)),
         send(n_hbm.at[:, 0:8, :], n.at[:, TOP + Y :, :], 6, (gx, down)),
         send(n_hbm.at[:, Y - 8 :, :], n.at[:, 0:TOP, :], 7, (gx, up)),
-    ]
+    ] + rows_of(0, 4)
     for copy in halo0[:2] + halo0[4:] + halo0[2:4]:
         copy.start()
     for who in gy_two:
         pl.semaphore_signal(z_sem, inc=1, device_id=who, device_id_type=MESH)
-    halo1 = exchange(p1, [alone.at[i : i + 1] for i in range(4)], 8)
-    halo2 = exchange(p2, [p2.at[a : a + 1, OWN, :] for a in (2, 9, 3, 8)], 14)
+    halo2 = exchange(p2, 2, [p2.at[a : a + 1, OWN, :] for a in (2, 9, 3, 8)], 18)
+    halo1 = [
+        send(alone.at[i : i + 1, 8 : Y - 8, :], p1.at[to : to + 1, TOP + 8 : TOP + Y - 8, :], at, who)
+        for at, (i, to, who) in enumerate(
+            ((0, 10, (left, gy)), (3, 1, (right, gy)), (1, 11, (left, gy)), (2, 0, (right, gy))), 8
+        )
+    ]
+    halo1 += rows_of(1, 12)
+    halo1 += [
+        send(
+            alone.at[i : i + 2, row : row + 8, :],
+            p1.at[to : to + 2, TOP + row : TOP + row + 8, :],
+            at,
+            who,
+        )
+        for at, (i, to, row, who) in enumerate(
+            (
+                (0, 10, 0, (left, gy)),
+                (2, 0, 0, (right, gy)),
+                (0, 10, Y - 8, (left, gy)),
+                (2, 0, Y - 8, (right, gy)),
+            ),
+            14,
+        )
+    ]
 
     loads[3].wait()
 
@@ -310,33 +345,46 @@
 
     def inside(p):
         move_east(p, e, e, range(2, 8))
-        move_north(p, n, TOP + 8, TOP + Y - 8)
-
-    def north_edges(p, halo):
-        for copy in halo[4:]:
+        move_north(p, n, TOP + 1, TOP + Y - 1)
+
+    def north_edges(p, k, copies):
+        for copy in copies:
             copy.wait()
+        unpack_rows(rows_in.at[k], p)
         edges_north(p, n)
 
     inside(p0)
-    north_edges(p0, halo0)
     e[1] = e[1] - 0.5 * p0[3, OWN, :]
     e[8] = e[8] + 0.5 * p0[8, OWN, :]
-
-    def by_itself(which, at):
-        forcing = jnp.concatenate([v[a] + BUOYANCY * th[a] for a in which], axis=0)
+    slot = {0: 0, 1: 1, 6: 2, 7: 3}
+
+    def by_itself(parts):
+        forcing = [v[a, low:high] + BUOYANCY * th[a, low:high] for a, low, high in parts]
         q = []
-        for a in which:
-            west = -0.5 * p0[2, OWN, :] if a == 0 else e[a]
-            east = 0.5 * p0[9, OWN, :] if a == 7 else e[a + 2]
-            q.append(explicit_pressure(p0, east, west, n, c, a))
-        vertical, pressure = solve(forcing, jnp.concatenate(q, axis=0), wh[...], wl[...])
-        for i, a in enumerate(which):
-            v[a] = vertical[i * Y : (i + 1) * Y]
-            alone[at + i] = pressure[i * Y : (i + 1) * Y]
-            halo1[at + i].start()
-
-    by_itself((0, 7), 0)
-    by_itself((1, 6), 2)
+        for a, low, high in parts:
+            rows = slice(TOP + low, TOP + high)
+            west = -0.5 * p0[2, rows, :] if a == 0 else e[a, low:high]
+            east = 0.5 * p0[9, rows, :] if a == 7 else e[a + 2, low:high]
+            q.append(explicit_pressure(p0, east, west, n, c, a, low, high))
+        vertical, pressure = solve(
+            jnp.concatenate(forcing, axis=0), jnp.concatenate(q, axis=0), wh[...], wl[...]
+        )
+        at = 0
+        for a, low, high in parts:
+            v[a, low:high] = vertical[at : at + high - low]
+            alone[slot[a], low:high] = pressure[at : at + high - low]
+            at += high - low
+
+    by_itself([(a, 8, Y - 8) for a in (0, 7)])
+    halo1[0].start()
+    halo1[1].start()
+    by_itself([(a, 8, Y - 8) for a in (1, 6)])
+    halo1[2].start()
+    halo1[3].start()
+    north_edges(p0, 0, halo0[4:])
+    by_itself([(a, low, low + 8) for a in (0, 1, 6, 7) for low in (0, Y - 8)])
+    for copy in halo1[6:]:
+        copy.start()
     planes(p0, p1, (2, 3, 4, 5), False)
 
     def added_pressure(planes_of_q):
@@ -362,7 +410,8 @@
     )
     for i, a in enumerate((0, 7, 1, 6)):
         v[a] = v[a] + vertical[i * Y : (i + 1) * Y]
-        p1[a + 2, OWN, :] = alone[i] + pressure[i * Y : (i + 1) * Y]
+        p1[a + 2, OWN, :] = alone[slot[a]] + pressure[i * Y : (i + 1) * Y]
+    pack_rows(p1, rows_out.at[1])
     halo1[4].start()
     halo1[5].start()
     e[0] = e[0] - 0.5 * p0[2, OWN, :]
@@ -384,8 +433,8 @@
     th_low[...] = low
 
     inside(p1)
-    north_edges(p1, halo1)
-    for copy in halo1[:4]:
+    north_edges(p1, 1, halo1[4:6])
+    for copy in halo1[:4] + halo1[6:]:
         copy.wait()
     e[0] = e[0] - 0.5 * (p1[2, OWN, :] - (p1[0, OWN, :] + spill[0]))
     e[1] = e[1] - 0.5 * (p1[3, OWN, :] - (p1[1, OWN, :] + spill[1]))
@@ -406,11 +455,12 @@
     for copy in stage3:
         copy.start()
     planes(p1, p2, (2, 3, 4, 5), True)
+    pack_rows(p2, rows_out.at[2])
     for copy in halo2[4:]:
         copy.start()
 
     inside(p2)
-    north_edges(p2, halo2)
+    north_edges(p2, 2, halo2[4:])
     which = (2, 3, 4, 5)
     forcing = jnp.concatenate([f[a] for a in which], axis=0)
     q = jnp.concatenate([explicit_pressure(p2, e[a + 2], e[a], n, c, a) for a in which], axis=0)
@@ -516,6 +566,8 @@
             pltpu.VMEM((2, Y, Z), F32),
             pltpu.VMEM((4, Y, Z), F32),
             pltpu.VMEM((4, Y, Z), F32),
+            pltpu.VMEM((3, 2, 2, X, Z), F32),
+            pltpu.VMEM((3, 2, 2, X, Z), F32),
             pltpu.VMEM((Z, 2 * Z), BF16),
             pltpu.VMEM((Z, 2 * Z), BF16),
             pltpu.VMEM((lo_size, 8, Z), F32),
@@ -524,8 +576,8 @@
             dma((8,)),
             dma((CHUNKS,)),
             dma((CHUNKS,)),
-            dma((20,)),
-            dma((20,)),
+            dma((24,)),
+            dma((24,)),
             dma((peers,)),
             dma((peers,)),
             pltpu.SemaphoreType.REGULAR,

time: 27.7 us -> 27.4 us (0.989)
  Pallas kernels: 26.8 us -> 26.3 us
    pallas_call x1, Pallas kernels: 23.7 us -> 23.2 us  [local(): pl.pallas_call(functools.partial(kernel_main, lo_size), out_shape=tuple((...]
where the time goes in v4:
time: 27.4 us; the launch traced here: 26.9 us
  Pallas kernels  26.3 us (96%)
  between operations  0.66 us (2%)
    pallas_call x1, Pallas kernels, local(): pl.pallas_call(functools.partial(kernel_main, lo_size), out_shape=tuple((...  23.2 us
    pallas_call x1, Pallas kernels, local(): pl.pallas_call(kernel_last, out_shape=(grid,) * 6 + (jax.ShapeDtypeStruct...  3.07 us

profile of v4, /device:TPU:32, one launch (start us, length us, event | category | flops | bytes accessed | tf_op | source)
XLA Modules:
  0.0 26.9 jit_solution(9890256378331864140)
XLA Ops:
  0.6 0.0 copy-start
  0.6 23.2 %condense_and_step.1 = (f32[12,144,128]{2,1,0:T(8,128)S(1)}, f32[10,128,128]{2,1,0:T(8,128)S(1)}, f32[8,144,128]{2,1,0:T(8,128)S(1)}, f32[8,128,128]{2,1,0:T(8,1...) custom-call(f32[8,128,128]{2,1,0:T(8,128)} %e_hbm.1, ...), custom_call_target="tpu_custom_call" | custom-call | tf_op jit(solution)/shard_map/condense_and_step/pallas_call | solution.py:552
  23.9 0.0 copy-done
  23.9 3.1 %last_step.1 = (f32[8,128,128]{2,1,0:T(8,128)}, f32[8,128,128]{2,1,0:T(8,128)}, f32[8,128,128]{2,1,0:T(8,128)}, f32[8,128,128]{2,1,0:T(8,128)}, f32[8,128,128]{2...) custom-call(f32[12,144,128]{2,1,0:T(8,128)S(1)} %get-tuple-element.28.p, ...), custom_call_target="tpu_custom_call" | custom-call | tf_op jit(solution)/shard_map/last_step/pallas_call | solution.py:591
Async XLA Ops:
  0.6 23.2 %copy-start = (f32[128]{0:T(128)S(1)}, f32[128]{0:T(128)}, u32[]{:S(2)}) copy-start(f32[128]{0:T(128)} %param.16) | copy-start | bytes 1540

commit v5 on v4

--- a/solution.py
+++ b/solution.py
@@ -108,8 +108,8 @@
 def kernel_main(
     lo_size,
     e_hbm, n_hbm, v_hbm, p_hbm, th_hbm, hu_hbm, c_hbm, r_hbm, m_hbm, k_hbm,
-    p2, e, n, f, th, hu, r, wh, wl, v_new, p_new, total,
-    p0, p1, v, c_ref, m_ref, k_ref, cl, xr, a_ref, alone, spill, rows_out, rows_in, th_high, th_low, r1, r2, r3,
+    p2, e, n, f, th, hu, r, wh, wl, v_new, p_new, total, th_high, th_low,
+    p0, p1, v, c_ref, m_ref, k_ref, cl, xr, a_ref, alone, spill, rows_out, rows_in, r1, r2, r3,
     load_sem, r_sem, m_sem, hs, hr, as_, ar, z_sem,
 ):
     gx, gy = lax.axis_index("gx"), lax.axis_index("gy")
@@ -470,19 +470,15 @@
 
     for copy in stage3:
         copy.wait()
-    mean = add(r3, ny) * (1.0 / (nx * X * ny * Y))
-    pull = times(jnp.concatenate([mean, mean], axis=0), th_high[...], th_low[...])[1:2, :]
-    v_new[...] = v_new[...] + pull[:, :Z]
-    p_new[...] = p_new[...] + pull[:, Z:]
-    total[...] = jnp.where(row == 0, mean, jnp.where(row == 1, pull[:, :Z], pull[:, Z:]))
+    total[...] = add(r3, ny) * (1.0 / (nx * X * ny * Y))
     for copy in halo2[:4]:
         copy.wait()
 
 
 def kernel_last(
-    p, e, n, f, th, hu, r, wh, wl, v_in, p_in, total, c_ref,
+    p, e, n, f, th, hu, r, wh, wl, v_in, p_in, total, th_high, th_low, c_ref,
     e_out, n_out, v_out, p_out, th_out, hu_out, r_out, s_out,
-    e_new, v_new, p_new, sem,
+    e_new, v_new, p_new, v_mid, p_mid, sem,
 ):
     copies = []
 
@@ -496,11 +492,14 @@
     out(hu, hu_out)
     out(n.at[:, OWN, :], n_out)
     out(e.at[2:8], e_out.at[1:7])
-    out(v_in, v_out.at[2:6])
-    out(p_in, p_out.at[2:6])
     c = c_ref[...]
-    stats = total[...]
-    s_out[...] = stats[0:1, :]
+    mean = total[...]
+    s_out[...] = mean[0:1, :]
+    pull = times(jnp.concatenate([mean, mean], axis=0), th_high[...], th_low[...])[1:2, :]
+    v_mid[...] = v_in[...] + pull[:, :Z]
+    p_mid[...] = p_in[...] + pull[:, Z:]
+    out(v_mid, v_out.at[2:6])
+    out(p_mid, p_out.at[2:6])
     for at, a in enumerate((0, 1, 8, 9)):
         e_new[at] = e[a] - 0.5 * (p[a + 2, OWN, :] - p[a, OWN, :])
     out(e_new.at[1:2], e_out.at[0:1])
@@ -516,8 +515,8 @@
         axis=0,
     )
     vertical, pressure = solve(forcing, q, wh[...], wl[...])
-    v_new[...] = (vertical + stats[1:2, :]).reshape(4, Y, Z)
-    p_new[...] = (pressure + stats[2:3, :]).reshape(4, Y, Z)
+    v_new[...] = (vertical + pull[:, :Z]).reshape(4, Y, Z)
+    p_new[...] = (pressure + pull[:, Z:]).reshape(4, Y, Z)
     out(v_new.at[0:2], v_out.at[0:2])
     out(p_new.at[0:2], p_out.at[0:2])
     out(v_new.at[2:4], v_out.at[6:8])
@@ -548,6 +547,8 @@
         ((4, Y, Z), F32),
         ((4, Y, Z), F32),
         ((8, Z), F32),
+        ((Z, 2 * Z), BF16),
+        ((Z, 2 * Z), BF16),
     ]
     state = pl.pallas_call(
         functools.partial(kernel_main, lo_size),
@@ -568,8 +569,6 @@
             pltpu.VMEM((4, Y, Z), F32),
             pltpu.VMEM((3, 2, 2, X, Z), F32),
             pltpu.VMEM((3, 2, 2, X, Z), F32),
-            pltpu.VMEM((Z, 2 * Z), BF16),
-            pltpu.VMEM((Z, 2 * Z), BF16),
             pltpu.VMEM((lo_size, 8, Z), F32),
             pltpu.VMEM((nx // lo_size, 8, Z), F32),
             pltpu.VMEM((ny, 8, Z), F32),
@@ -603,6 +602,8 @@
             pltpu.VMEM((4, Y, Z), F32),
             pltpu.VMEM((4, Y, Z), F32),
             pltpu.VMEM((4, Y, Z), F32),
+            pltpu.VMEM((4, Y, Z), F32),
+            pltpu.VMEM((4, Y, Z), F32),
             dma((13,)),
         ],
         compiler_params=pltpu.CompilerParams(vmem_limit_bytes=24 << 20),

time: 27.4 us -> 27.2 us (level)
  no operation moved by 1% of the time
where the time goes in v5:
time: 27.2 us; the launch traced here: 26.8 us
  Pallas kernels  26.1 us (96%)
  between operations  0.66 us (2%)
    pallas_call x1, Pallas kernels, local(): pl.pallas_call(functools.partial(kernel_main, lo_size), out_shape=tuple((...  23 us
    pallas_call x1, Pallas kernels, local(): pl.pallas_call(kernel_last, out_shape=(grid,) * 6 + (jax.ShapeDtypeStruct...  3.07 us

profile of v5, /device:TPU:32, one launch (start us, length us, event | category | flops | bytes accessed | tf_op | source)
XLA Modules:
  0.0 26.8 jit_solution(15362691999124025573)
XLA Ops:
  0.6 0.0 copy-start
  0.6 23.0 %condense_and_step.1 = (f32[12,144,128]{2,1,0:T(8,128)S(1)}, f32[10,128,128]{2,1,0:T(8,128)S(1)}, f32[8,144,128]{2,1,0:T(8,128)S(1)}, f32[8,128,128]{2,1,0:T(8,1...) custom-call(f32[8,128,128]{2,1,0:T(8,128)} %e_hbm.1, ...), custom_call_target="tpu_custom_call" | custom-call | tf_op jit(solution)/shard_map/condense_and_step/pallas_call | solution.py:553
  23.7 0.0 copy-done
  23.7 3.1 %last_step.1 = (f32[8,128,128]{2,1,0:T(8,128)}, f32[8,128,128]{2,1,0:T(8,128)}, f32[8,128,128]{2,1,0:T(8,128)}, f32[8,128,128]{2,1,0:T(8,128)}, f32[8,128,128]{2...) custom-call(f32[12,144,128]{2,1,0:T(8,128)S(1)} %get-tuple-element.30.p, ...), custom_call_target="tpu_custom_call" | custom-call | tf_op jit(solution)/shard_map/last_step/pallas_call | solution.py:590
Async XLA Ops:
  0.6 23.1 %copy-start = (f32[128]{0:T(128)S(1)}, f32[128]{0:T(128)}, u32[]{:S(2)}) copy-start(f32[128]{0:T(128)} %param.16) | copy-start | bytes 1540
